TPU v7x, 256 devices: a whole 4x4x8 slice. The times are simulated.
256 devices in a mesh: tp: 4 (over y), ep: 64 (over x, z, core).
Axes of the slice: x: 4, y: 4, z: 8, core: 2. Of those that a mesh axis runs over, the one named last changes fastest.
Arguments:
- queries: bfloat16 [2048, 64, 128], P('ep', 'tp'), may hold values from -6 to 6
- cache_keys: bfloat16 [2048, 4, 192, 128], P('ep', 'tp'), may hold values from -6 to 6
- cache_values: bfloat16 [2048, 4, 192, 128], P('ep', 'tp'), may hold values from -6 to 6
- new_keys: bfloat16 [2048, 4, 128], P('ep', 'tp'), may hold values from -6 to 6
- new_values: bfloat16 [2048, 4, 128], P('ep', 'tp'), may hold values from -6 to 6
- lengths: int32 [2048], P('ep'), may hold values from 1 to 192, as said below
- out_weight: bfloat16 [8192, 4096], P('tp', 'ep'), may hold values from -0.25 to 0.25
- residual: bfloat16 [64, 32, 4096], P('ep', 'tp'), may hold values from -6 to 6
- norm_gain: bfloat16 [4096], replicated, may hold values from 0.25 to 1.75
- routes: int32 [64, 32, 8], P('ep', 'tp'), may hold values from 0 to 63, all different within a row; in each aligned block of 8 rows (0 to 7, 8 to 15, ..., all dimensions but the last counted through in order) at most 2 rows name the same one
- route_weights: float32 [64, 32, 8], P('ep', 'tp'), may hold values from 0.1 to 0.6
- gate_weight: bfloat16 [64, 4096, 1536], P('ep', None, 'tp'), may hold values from -0.09375 to 0.09375
- up_weight: bfloat16 [64, 4096, 1536], P('ep', None, 'tp'), may hold values from -0.09375 to 0.09375
- down_weight: bfloat16 [64, 1536, 4096], P('ep', 'tp'), may hold values from -0.15625 to 0.15625
Outputs:
- layer_out: bfloat16 [64, 32, 4096], P('ep', 'tp')
Inputs may be any that keep to these rules, and one draw needn't show every extreme that they name: `lengths`: every decode group of 32 rows has at least one row with all 192 cache slots valid. `routes`: each row names 8 different experts; among the rows of one device (aligned blocks of 8 rows in row order) no expert is named by more than 2 rows, a bound that some block reaches.
All inputs are finite; a program needn't handle non-finite values.
Results may differ from a plain program's by a relative error of at most 0.017.
Values may be sent and summed in bfloat16 or wider, within the bound.
A program may use at most 128 MiB of HBM per device.

v0:
```python
import jax
import jax.numpy as jnp
from jax import lax
from jax.sharding import PartitionSpec as P


def run_expert(arrived, gate_w, up_w, down_w):
    gate = jnp.dot(arrived, gate_w, preferred_element_type=jnp.float32)
    up = jnp.dot(arrived, up_w, preferred_element_type=jnp.float32)
    act = (jax.nn.silu(gate) * up).astype(jnp.bfloat16)
    part_sum = jnp.dot(act, down_w, preferred_element_type=jnp.float32)
    return lax.optimization_barrier(part_sum.astype(jnp.bfloat16))


def on_device(
    queries,
    cache_keys,
    cache_values,
    new_keys,
    new_values,
    lengths,
    out_weight,
    residual,
    norm_gain,
    routes,
    route_weights,
    gate_weight,
    up_weight,
    down_weight,
):
    count = queries.shape[0]
    group = queries.shape[1]
    width = queries.shape[2]
    scale = width ** (-0.5)
    keys_here = cache_keys[:, 0]
    values_here = cache_values[:, 0]
    cached = (
        jnp.einsum("rgd,rcd->rgc", queries, keys_here, preferred_element_type=jnp.float32) * scale
    )
    fresh = (
        jnp.einsum("rgd,rd->rg", queries, new_keys[:, 0], preferred_element_type=jnp.float32)
        * scale
    )
    valid = (jnp.arange(keys_here.shape[1], dtype=jnp.int32)[None, :] < lengths[:, None])[
        :, None, :
    ]
    cached = jnp.where(valid, cached, jnp.float32(-1e30))
    peak = jnp.maximum(jnp.max(cached, axis=-1), fresh)
    cached_w = jnp.where(valid, jnp.exp(cached - peak[..., None]), jnp.float32(0.0))
    fresh_w = jnp.exp(fresh - peak)
    total = jnp.sum(cached_w, axis=-1) + fresh_w
    cached_p = (cached_w / total[..., None]).astype(jnp.bfloat16)
    fresh_p = lax.optimization_barrier((fresh_w / total).astype(jnp.bfloat16))
    mixed = jnp.einsum("rgc,rcd->rgd", cached_p, values_here, preferred_element_type=jnp.float32)
    mixed = (
        mixed
        + fresh_p.astype(jnp.float32)[..., None] * new_values[:, 0].astype(jnp.float32)[:, None, :]
    )
    attn_flat = mixed.astype(jnp.bfloat16).reshape(count, group * width)
    partial_value = jnp.dot(
        lax.all_gather(attn_flat, "ep", axis=0, tiled=True),
        out_weight,
        preferred_element_type=jnp.float32,
    )
    ep_size = lax.axis_size("ep")
    tp_size = lax.axis_size("tp")
    owned = count // tp_size
    partial_value = partial_value.reshape(ep_size, tp_size, owned, partial_value.shape[1])
    mine = lax.psum_scatter(
        partial_value.astype(jnp.bfloat16), "tp", scatter_dimension=1, tiled=True
    )
    assembled = lax.all_to_all(mine, "ep", split_axis=0, concat_axis=3, tiled=True)
    model_width = assembled.shape[3]
    hidden = residual[0].astype(jnp.float32) + assembled.reshape(owned, model_width).astype(
        jnp.float32
    )
    inverse = lax.rsqrt(jnp.mean(hidden * hidden, axis=-1, keepdims=True) + 1e-06)
    normed = (hidden * inverse * norm_gain.astype(jnp.float32)[None, :]).astype(jnp.bfloat16)
    chosen = routes[0]
    shares = route_weights[0]
    top = chosen.shape[1]
    capacity = max(2, min(owned, (owned * top + ep_size - 1) // ep_size + 1))
    onehot = chosen[:, :, None] == jnp.arange(ep_size, dtype=jnp.int32)[None, None, :]
    member = jnp.sum(onehot.astype(jnp.int32), axis=1)
    rank = jnp.cumsum(member, axis=0) - member
    place = (rank[:, :, None] == jnp.arange(capacity, dtype=jnp.int32)[None, None, :]) & (
        member[:, :, None] > 0
    )
    share = jnp.sum(jnp.where(onehot, shares[:, :, None], jnp.float32(0.0)), axis=1)
    outgoing = jnp.einsum(
        "rxc,rd->xcd", place.astype(jnp.bfloat16), normed, preferred_element_type=jnp.float32
    ).astype(jnp.bfloat16)
    gate_w = gate_weight[0]
    up_w = up_weight[0]
    down_w = down_weight[0]
    stacked = lax.all_gather(outgoing[:, None], "tp", axis=1, tiled=True)
    arrived = lax.all_to_all(stacked, "ep", split_axis=0, concat_axis=0, tiled=True)
    worked = run_expert(arrived.reshape(-1, model_width), gate_w, up_w, down_w).reshape(
        arrived.shape
    )
    returned = lax.all_to_all(worked, "ep", split_axis=0, concat_axis=0, tiled=True)
    summed = lax.psum_scatter(
        returned.astype(jnp.float32).astype(jnp.bfloat16), "tp", scatter_dimension=1, tiled=True
    ).astype(jnp.float32)
    expert_out = summed[:, 0].astype(jnp.bfloat16)
    coefficient = jnp.where(place, share[:, :, None], jnp.float32(0.0))
    moe = jnp.einsum(
        "rxc,xcd->rd", coefficient, expert_out.astype(jnp.float32), precision=lax.Precision.HIGHEST
    )
    return (hidden + moe).astype(jnp.bfloat16)[None]


def solution(mesh):
    placed = (
        P("ep", "tp", None),
        P("ep", "tp", None, None),
        P("ep", "tp", None, None),
        P("ep", "tp", None),
        P("ep", "tp", None),
        P("ep"),
        P("tp", "ep"),
        P("ep", "tp", None),
        P(),
        P("ep", "tp", None),
        P("ep", "tp", None),
        P("ep", None, "tp"),
        P("ep", None, "tp"),
        P("ep", "tp", None),
    )
    return jax.shard_map(
        on_device, mesh=mesh, in_specs=placed, out_specs=P("ep", "tp", None), check_vma=False
    )
```

profile of v0, /device:TPU:1, one launch (start us, length us, event | category | flops | bytes accessed | tf_op | source)
XLA Modules:
  0.0 531.3 jit_solution(11654085204174163809)
XLA Ops:
  6.5 0.9 iota_compare_fusion.1
  7.4 1.2 fusion.43
  8.6 2.5 fusion.59
  11.2 0.3 fusion.33
  11.5 0.6 fusion.27
  12.1 0.7 copy.41
  12.9 87.3 %all-gather.4.cloned.1.call-done = bf16[2048,2048]{1,0:T(8,128)(2,1)} async-done(((bf16[32,2048]{1,0:T(8,128)(2,1)}), bf16[2048,2048]{1,0:T(8,128)(2,1)}) %all-gather.4.cloned.1.call-update) | async-done | bytes 8388624 | tf_op jit(solution)/shard_map/all_gather | solution.py:61
  100.2 6.0 %convolution_convert_fusion.2 = bf16[2048,64]{0,1:T(8,128)(2,1)S(1)} fusion(bf16[2048,2048]{1,0:T(8,128)(2,1)} %all-gather.4.cloned.1.call-done, bf16[2048,64]{0,1:T(8,128)(2,1)} %param.20), kind=kOutput, calls=%fused_computation.11 | convolution fusion | flops 537001984 | bytes 8912896 | tf_op jit(solution)/shard_map/dot_general | solution.py:60
  106.2 1.0 copy.29
  107.4 0.6 sub.21
  108.0 0.6 dynamic-slice
  108.6 42.0 %all-reduce.3.cloned.1.call-done = bf16[64,4,8,64]{3,2,1,0:T(8,128)(2,1)} async-done(((bf16[64,4,8,64]{3,2,1,0:T(8,128)(2,1)}), bf16[64,4,8,64]{3,2,1,0:T(8,128)(2,1)}) %all-reduce.3.cloned.1.call-update) | async-done | bytes 262160
  150.6 1.6 constant_dynamic-slice_fusion
  152.1 0.8 reshape.80
  152.9 12.5 %all-to-all-start = ((bf16[64,2,256]{2,1,0:T(2,128)(2,1)}), bf16[64,2,256]{2,1,0:T(2,128)(2,1)S(1)}, u32[]{:S(2)}, u32[]{:S(2)}) async-start(bf16[64,2,256]{2,1,0:T(2,128)(2,1)} %reshape.80), calls=%async_computation | async-start | bytes 131072 | tf_op jit(solution)/shard_map/all_to_all | solution.py:72
  165.4 0.5 broadcast_compare_fusion
  166.0 9.2 %all-to-all-done = bf16[64,2,256]{2,1,0:T(2,128)(2,1)S(1)} async-done(((bf16[64,2,256]{2,1,0:T(2,128)(2,1)}), bf16[64,2,256]{2,1,0:T(2,128)(2,1)S(1)}, u32[]{:S(2)}, u32[]{:S(2)}) %all-to-all-start) | async-done | bytes 65568 | tf_op jit(solution)/shard_map/all_to_all | solution.py:72
  175.2 0.1 reshape.81
  175.5 1.0 multiply_reduce_fusion
  176.5 2.3 convolution_convert_fusion.1
  178.9 45.0 %all-gather.6.cloned.1.call-done = bf16[64,8,4096]{2,0,1:T(8,128)(2,1)} async-done(((bf16[64,2,4096]{2,0,1:T(8,128)(2,1)}), bf16[64,8,4096]{2,0,1:T(8,128)(2,1)}) %all-gather.6.cloned.1.call-update) | async-done | bytes 4194320 | tf_op jit(solution)/shard_map/all_gather | solution.py:96
  223.9 8.5 %copy.31 = bf16[64,4,2,4096]{3,2,1,0:T(2,128)(2,1)} copy(bf16[64,4,2,4096]{3,0,2,1:T(8,128)(2,1)} %bitcast.88) | data formatting | bytes 8388608 | tf_op jit(solution)/shard_map/all_gather | solution.py:96
  232.4 106.9 %all_to_all.19 = bf16[64,4,2,4096]{3,2,1,0:T(2,128)(2,1)} all-to-all(bf16[64,4,2,4096]{3,2,1,0:T(2,128)(2,1)} %copy.31), channel_id=1, replica_groups=mesh['tp'=4,'ep'=64] {'ep'}, dimensions={0} | all-to-all | bytes 8388608 | tf_op jit(solution)/shard_map/all_to_all | solution.py:97
  339.4 7.2 %reshape.66 = bf16[512,4096]{1,0:T(8,128)(2,1)} reshape(bf16[64,4,2,4096]{3,2,1,0:T(2,128)(2,1)} %all_to_all.19) | data formatting | bytes 8388608 | tf_op jit(solution)/shard_map/reshape | solution.py:98
  346.6 6.4 %fusion.6 = f32[512,384]{1,0:T(8,128)} fusion(bf16[512,4096]{1,0:T(8,128)(2,1)} %reshape.66, bf16[1,4096,384]{2,1,0:T(8,128)(2,1)} %param.25), kind=kOutput, calls=%fused_computation.9 | convolution fusion | flops 1610612736 | bytes 8126464 | tf_op jit(solution)/shard_map/dot_general | solution.py:8
  353.0 9.8 %convolution_convert_fusion = bf16[512,4096]{1,0:T(8,128)(2,1)} fusion(bf16[1,384,4096]{2,1,0:T(8,128)(2,1)S(1)} %copy-done, bf16[512,4096]{1,0:T(8,128)(2,1)} %reshape.66, bf16[1,4096,384]{2,1,0:T(8,128)(2,1)} %param.26, f32[512,384]{1,0:T(8,128)} %fusion.6), kind=kOutput, calls=%fused_computation | convolution fusion | flops 3224502272 | bytes 15466496 | tf_op jit(solution)/shard_map/dot_general | solution.py:11
  362.7 7.6 %reshape.67 = bf16[64,4,2,4096]{3,2,1,0:T(2,128)(2,1)} reshape(bf16[512,4096]{1,0:T(8,128)(2,1)} %convolution_convert_fusion) | data formatting | bytes 8388608 | tf_op jit(solution)/shard_map/reshape | solution.py:98
  370.3 102.0 %all_to_all.20 = bf16[64,4,2,4096]{3,2,1,0:T(2,128)(2,1)S(1)} all-to-all(bf16[64,4,2,4096]{3,2,1,0:T(2,128)(2,1)} %reshape.67), channel_id=1, replica_groups=mesh['tp'=4,'ep'=64] {'ep'}, dimensions={0} | all-to-all | bytes 8388608 | tf_op jit(solution)/shard_map/all_to_all | solution.py:101
  472.3 4.8 copy.32
  477.2 0.6 copy-done.4
  478.0 44.4 %reduce-scatter.3.cloned.1.call-done = bf16[64,1,2,4096]{3,0,2,1:T(8,128)(2,1)} async-done(((bf16[64,4,2,4096]{3,0,2,1:T(8,128)(2,1)}), bf16[64,1,2,4096]{3,0,2,1:T(8,128)(2,1)}) %reduce-scatter.3.cloned.1.call-update) | async-done | bytes 1048592 | tf_op jit(solution)/shard_map/reduce_scatter | solution.py:102
  522.4 2.4 fusion.2
  (41 shorter events, 0.7 us)
Async XLA Ops:
  6.5 346.5 %copy-start = (bf16[1,384,4096]{2,1,0:T(8,128)(2,1)S(1)}, bf16[1,384,4096]{2,1,0:T(8,128)(2,1)}, u32[]{:S(2)}) copy-start(bf16[1,384,4096]{2,1,0:T(8,128)(2,1)} %param.27) | copy-start | bytes 9437188
  6.5 4.9 copy-start.6
  6.5 93.6 %all-gather.4.cloned.1.call-start = ((), (), s32[]{:S(2)}) async-start(), calls=%async_computation.4 | async-start | bytes 8519680 | tf_op jit(solution)/shard_map/all_gather | solution.py:61
  6.5 4.9 copy-start.9
  12.8 94.4 %copy-start.3 = (s32[1,8,8]{2,1,0:T(8,128)S(1)}, s32[1,8,8]{2,1,0:T(8,128)}, u32[]{:S(2)}) copy-start(s32[1,8,8]{2,1,0:T(8,128)} %param.23) | copy-start | bytes 772
  12.8 95.1 %copy-start.7 = (bf16[4096]{0:T(1024)(128)(2,1)S(1)}, bf16[4096]{0:T(1024)(128)(2,1)}, u32[]{:S(2)}) copy-start(bf16[4096]{0:T(1024)(128)(2,1)} %param.22) | copy-start | bytes 24580
  12.8 95.1 %copy-start.10 = (u32[256]{0:T(256)S(1)}, u32[256]{0:T(256)}, u32[]{:S(2)}) copy-start(u32[256]{0:T(256)} %constant.37) | copy-start | bytes 3076
  12.8 137.7 %all-reduce.3.cloned.1.call-start = ((), (), s32[]{:S(2)}) async-start(), calls=%async_computation.7 | async-start | bytes 1048576
  152.9 22.3 %all-to-all-start = ((bf16[64,2,256]{2,1,0:T(2,128)(2,1)}), bf16[64,2,256]{2,1,0:T(2,128)(2,1)S(1)}, u32[]{:S(2)}, u32[]{:S(2)}) async-start(bf16[64,2,256]{2,1,0:T(2,128)(2,1)} %reshape.80), calls=%async_computation | async-start | bytes 131072 | tf_op jit(solution)/shard_map/all_to_all | solution.py:72
  165.4 58.5 %all-gather.6.cloned.1.call-start = ((), (), s32[]{:S(2)}) async-start(), calls=%async_computation.6 | async-start | bytes 5242880 | tf_op jit(solution)/shard_map/all_gather | solution.py:96
  178.9 343.5 %reduce-scatter.3.cloned.1.call-start = ((), (), s32[]{:S(2)}) async-start(), calls=%async_computation.5 | async-start | bytes 5242880 | tf_op jit(solution)/shard_map/reduce_scatter | solution.py:102
  477.2 0.7 copy-start.4
  477.2 0.7 copy-start.8
  477.2 45.2 %copy-start.1 = (bf16[1,8,4096]{2,1,0:T(8,128)(2,1)S(1)}, bf16[1,8,4096]{2,1,0:T(8,128)(2,1)}, u32[]{:S(2)}) copy-start(bf16[1,8,4096]{2,1,0:T(8,128)(2,1)} %param.21) | copy-start | bytes 196612
  477.2 45.2 %copy-start.2 = (s32[8,64]{1,0:T(8,128)S(1)}, s32[8,64]{1,0:T(8,128)}, u32[]{:S(2)}) copy-start(s32[8,64]{1,0:T(8,128)} %sub.21) | copy-start | bytes 6148
  477.2 45.2 %copy-start.5 = (pred[8,64]{1,0:T(8,128)(4,1)S(1)}, pred[8,64]{1,0:T(8,128)(4,1)}, u32[]{:S(2)}) copy-start(pred[8,64]{1,0:T(8,128)(4,1)} %broadcast_compare_fusion) | copy-start | bytes 1540
Sparse Core Ops, SparseCore 0:
  12.9 87.1 all-gather.3
  107.3 43.1 all-reduce.2
  179.0 44.8 all-gather.5
  477.4 44.9 reduce-scatter.2
where the time goes:
time: 532 us; the launch traced here: 531 us
  waiting for transfers between devices  228 us (43%)
  blocking collectives  209 us (39%)
  local copies, waits for them, and re-layouts  33.8 us (6%)
  matrix products  31.3 us (6%)
  between operations  13.3 us (2%)
  starting transfers between devices  12.6 us (2%)
    all_to_all x1, blocking collectives, on_device(): lax.all_to_all(stacked, 'ep', split_axis=0, concat_axis=0, tiled=True)  107 us
    all_to_all x1, blocking collectives, on_device(): lax.all_to_all(worked, 'ep', split_axis=0, concat_axis=0, tiled=True)  102 us
    all_gather x1, waiting for transfers between devices, on_device(): lax.all_gather(attn_flat, 'ep', axis=0, tiled=True)  87.3 us
    all_gather x1, waiting for transfers between devices, on_device(): stacked = lax.all_gather(outgoing[:, None], 'tp', axis=1, tiled=True)  45 us
    reduce_scatter x1, waiting for transfers between devices, on_device(): lax.psum_scatter(returned.astype(jnp.float32).astype(jnp.bfloat16), 'tp',...  44.4 us
    unnamed x5, waiting for transfers between devices  42.1 us
    all_to_all x1, starting transfers between devices, on_device(): lax.all_to_all(mine, 'ep', split_axis=0, concat_axis=3, tiled=True)  12.5 us
  transfers between devices with their start and end apart: 5, of which 5 were waited for; matrix products, arithmetic and copies ran while one was open for 0% of the time, Pallas kernels for 0%

commit v1 on v0

v1 whole, which is shorter than its diff:
```python
import functools

import jax
import jax.numpy as jnp
from jax import lax
from jax.experimental import pallas as pl
from jax.experimental.pallas import tpu as pltpu
from jax.sharding import PartitionSpec as P

MESH = pl.DeviceIdType.MESH
BF16 = jnp.bfloat16
F32 = jnp.float32
EP_SHAPE = (4, 8, 2)
LANES = 128
CAP = 2
VMEM_LIMIT = 60 * 1024 * 1024


def dot(a, b):
    return jnp.dot(a, b, preferred_element_type=F32)


def dot_nt(a, b):
    return lax.dot_general(a, b, (((1,), (1,)), ((), ())), preferred_element_type=F32)


def rel(i):
    return ((i + 1) // 2) * (2 * (i % 2) - 1)


def kernel(
    dims,
    lengths_ref,
    nk_ref,
    nv_ref,
    gain_ref,
    routes_ref,
    shares_ref,
    q_hbm,
    k_hbm,
    v_hbm,
    wt_hbm,
    res_hbm,
    gate_hbm,
    up_hbm,
    down_hbm,
    out_ref,
    q_buf,
    k_buf,
    v_buf,
    mixed_buf,
    fresh_buf,
    wg,
    xg,
    rs_send,
    rs_recv,
    projg,
    resg,
    hid,
    info,
    comb,
    sel,
    xs,
    gu,
    dwg,
    actg,
    ret_send,
    ret_recv,
    fin_send,
    fin_recv,
    fy_send,
    fy_recv,
    load_sem,
    ring_ss,
    ring_rs,
    x_ss,
    x_rs,
    res_ss,
    res_rs,
    info_ss,
    info_rs,
    infoy_ss,
    infoy_rs,
    dw_ss,
    dw_rs,
    rs_ss,
    rs_rs,
    proj_ss,
    proj_rs,
    sel_ss,
    sel_rs,
    xs_ss,
    xs_rs,
    act_ss,
    act_rs,
    ret_ss,
    ret_rs,
    fin_ss,
    fin_rs,
    fy_ss,
    fy_rs,
):
    nx, nz, nc, nt = dims
    ns = nx * nc
    rows = res_hbm.shape[0]
    width = res_hbm.shape[1]
    quarter = width // nt
    group_rows = nt * rows
    heads, head_size = q_buf.shape[1], q_buf.shape[2]
    context = k_buf.shape[1]
    hidden_units = gate_hbm.shape[1]
    chunk = ns * CAP

    ep = lax.axis_index("ep")
    t = lax.axis_index("tp")
    x = ep // (nz * nc)
    z = (ep // nc) % nz
    c = ep % nc
    s = x * nc + c

    def z_peer(d):
        return {"ep": (x * nz + (z + d + nz) % nz) * nc + c, "tp": t}

    def s_index(d):
        return (s + d) % ns

    def s_peer(d):
        p = s_index(d)
        return {"ep": ((p // nc) * nz + z) * nc + p % nc, "tp": t}

    def t_index(d):
        return (t + d) % nt

    def t_peer(d):
        return {"ep": ep, "tp": t_index(d)}

    pending = []

    def send(src, dst, ss, rs, peer):
        copy = pltpu.make_async_remote_copy(
            src_ref=src, dst_ref=dst, send_sem=ss, recv_sem=rs, device_id=peer, device_id_type=MESH
        )
        copy.start()
        pending.append(copy)

    def arrive(dst, ss, rs):
        pltpu.make_async_remote_copy(
            src_ref=dst, dst_ref=dst, send_sem=ss, recv_sem=rs, device_id=t_peer(1), device_id_type=MESH
        ).wait_recv()

    barrier = pltpu.get_barrier_semaphore()
    partners = (
        [z_peer(d) for d in range(1, nz)]
        + [s_peer(d) for d in range(1, ns)]
        + [t_peer(d) for d in range(1, nt)]
    )
    for peer in partners:
        pl.semaphore_signal(barrier, inc=1, device_id=peer, device_id_type=MESH)

    def load(src, dst, n):
        copy = pltpu.make_async_copy(src, dst, load_sem.at[n])
        copy.start()
        return copy

    q_load = load(q_hbm, q_buf, 0)
    k_load = load(k_hbm, k_buf, 1)
    v_load = load(v_hbm, v_buf, 2)
    w_load = load(wt_hbm, wg.at[z], 3)
    r_load = load(res_hbm, resg.at[s], 4)
    g_load = load(gate_hbm, gu.at[:, pl.ds(0, hidden_units)], 5)
    u_load = load(up_hbm, gu.at[:, pl.ds(hidden_units, hidden_units)], 6)
    my_quarter = pl.ds(pl.multiple_of(t * quarter, LANES), quarter)
    d_load = load(down_hbm.at[:, my_quarter], dwg.at[t], 7)

    lane = lax.broadcasted_iota(jnp.int32, (rows, LANES), 1)
    row = lax.broadcasted_iota(jnp.int32, (rows, LANES), 0)
    member = jnp.zeros((rows, LANES), F32)
    share = jnp.zeros((rows, LANES), F32)
    routes = routes_ref[...]
    shares = shares_ref[...]
    for k in range(routes.shape[1]):
        hit = routes[:, k : k + 1] == lane
        member = jnp.where(hit, 1.0, member)
        share = share + jnp.where(hit, shares[:, k : k + 1], 0.0)
    rank = jnp.zeros((rows, LANES), F32)
    for j in range(rows - 1):
        rank = rank + jnp.where(row > j, member[j : j + 1, :], 0.0)
    info[t, s, 0] = jnp.where(member > 0.0, rank, -1.0)
    info[t, s, 1] = share

    pl.semaphore_wait(barrier, len(partners))

    half = nz // 2
    wrows = wt_hbm.shape[0]
    top, low = pl.ds(0, wrows // 2), pl.ds(wrows // 2, wrows // 2)

    def ring_step(j):
        right_block = (z - (j - 1) + nz) % nz
        left_block = (z + (j - 1)) % nz
        right_src = wt_hbm if j == 1 else wg.at[right_block]
        left_src = wt_hbm if j == 1 else wg.at[left_block]
        right_dst, left_dst = wg.at[right_block], wg.at[left_block]
        if j == half:
            right_src, right_dst = right_src.at[top], right_dst.at[top]
            left_src, left_dst = left_src.at[low], left_dst.at[low]
        send(right_src, right_dst, ring_ss.at[0, j - 1], ring_rs.at[0, j - 1], z_peer(1))
        send(left_src, left_dst, ring_ss.at[1, j - 1], ring_rs.at[1, j - 1], z_peer(-1))

    def ring_wait(j):
        from_left = wg.at[(z - j + nz) % nz]
        from_right = wg.at[(z + j) % nz]
        if j == half:
            from_left, from_right = from_left.at[top], from_right.at[low]
        arrive(from_left, ring_ss.at[0, j - 1], ring_rs.at[0, j - 1])
        arrive(from_right, ring_ss.at[1, j - 1], ring_rs.at[1, j - 1])

    ring_step(1)
    for d in range(1, ns):
        send(info.at[t, s], info.at[t, s], info_ss.at[d], info_rs.at[d], s_peer(d))
    for d in range(1, ns):
        send(res_hbm, resg.at[s], res_ss.at[d], res_rs.at[d], s_peer(d))
    for d in range(1, nt):
        p = t_index(d)
        part = pl.ds(pl.multiple_of(p * quarter, LANES), quarter)
        send(down_hbm.at[:, part], dwg.at[t], dw_ss.at[d], dw_rs.at[d], t_peer(d))

    fresh_buf[0, :, 0, :] = nk_ref[...].astype(F32)
    fresh_buf[1, :, 0, :] = nv_ref[...].astype(F32)
    q_load.wait()
    k_load.wait()
    v_load.wait()
    scale = head_size ** (-0.5)
    step_rows = 4

    def attend(g, carry):
        for j in range(step_rows):
            r = g * step_rows + j
            q = q_buf[r]
            scores = dot_nt(q, k_buf[r]) * scale
            fresh = (
                jnp.sum(q.astype(F32) * fresh_buf[0, r], axis=1, keepdims=True)
                * scale
            )
            valid = lax.broadcasted_iota(jnp.int32, (heads, context), 1) < lengths_ref[r]
            scores = jnp.where(valid, scores, -1e30)
            peak = jnp.maximum(jnp.max(scores, axis=1, keepdims=True), fresh)
            weight = jnp.where(valid, jnp.exp(scores - peak), 0.0)
            fresh_w = jnp.exp(fresh - peak)
            total = jnp.sum(weight, axis=1, keepdims=True) + fresh_w
            probs = (weight / total).astype(BF16)
            fresh_p = (fresh_w / total).astype(BF16).astype(F32)
            mixed_buf[r] = dot(probs, v_buf[r]) + fresh_p * fresh_buf[1, r]
        return carry

    lax.fori_loop(0, group_rows // step_rows, attend, 0)
    for h in range(heads):
        xg[s, :, h * head_size : (h + 1) * head_size] = mixed_buf[:, h, :].astype(BF16)
    for d in range(1, ns):
        send(xg.at[s], xg.at[s], x_ss.at[d], x_rs.at[d], s_peer(d))

    for j in range(1, half):
        ring_wait(j)
        ring_step(j + 1)

    for d in range(1, ns):
        arrive(info.at[t, s_index(-d + ns)], info_ss.at[d], info_rs.at[d])
    for d in range(1, nt):
        send(info.at[t], info.at[t], infoy_ss.at[d], infoy_rs.at[d], t_peer(d))

    picks = nz * chunk
    slot_no = lax.broadcasted_iota(jnp.int32, (picks, LANES), 0)
    at_z = (z + rel(slot_no // chunk) + nz) % nz
    expert = (x * nz + at_z) * nc + c
    spread = (lax.broadcasted_iota(jnp.int32, (picks, LANES), 1) == expert).astype(BF16)
    code = info[t, :, 0].reshape(ns * rows, LANES).astype(BF16)
    seen = dot_nt(spread, code)
    slot_no = lax.broadcasted_iota(jnp.int32, (picks, ns * rows), 0)
    row_no = lax.broadcasted_iota(jnp.int32, (picks, ns * rows), 1)
    pick = (
        (seen == (slot_no % CAP).astype(F32)) & (row_no // rows == (slot_no % chunk) // CAP)
    ).astype(BF16)

    w_load.wait()
    ring_wait(half)
    for d in range(1, ns):
        arrive(xg.at[s_index(-d + ns)], x_ss.at[d], x_rs.at[d])
    all_rows = xg[...].reshape(ns * group_rows, xg.shape[2])
    ncol = nz * wrows
    zstep = min(nz, 4)
    for b in range(nz // zstep):
        cols = wg[b * zstep : (b + 1) * zstep].reshape(zstep * wrows, wg.shape[2])
        part = dot_nt(all_rows, cols).reshape(ns, nt, rows, zstep * wrows)
        for tt in range(nt):
            rs_send[tt, :, b * zstep * wrows : (b + 1) * zstep * wrows] = (
                part[:, tt].reshape(ns * rows, zstep * wrows).astype(BF16)
            )
    for d in range(1, nt):
        send(rs_send.at[t_index(d)], rs_recv.at[t], rs_ss.at[d], rs_rs.at[d], t_peer(d))
    for d in range(1, nt):
        arrive(rs_recv.at[t_index(-d + nt)], rs_ss.at[d], rs_rs.at[d])
    proj = rs_send[t].astype(F32)
    for d in range(1, nt):
        proj = proj + rs_recv[t_index(d)].astype(F32)
    projg[s] = proj.astype(BF16)
    for d in range(1, ns):
        send(projg.at[s], projg.at[s], proj_ss.at[d], proj_rs.at[d], s_peer(d))
    r_load.wait()
    for d in range(1, ns):
        arrive(resg.at[s_index(-d + ns)], res_ss.at[d], res_rs.at[d])
    for d in range(1, ns):
        arrive(projg.at[s_index(-d + ns)], proj_ss.at[d], proj_rs.at[d])

    nrow = ns * rows
    left_half = lax.broadcasted_iota(jnp.int32, (nrow, LANES), 1) < wrows
    squares = jnp.zeros((nrow, LANES), F32)
    for xx in range(nx):
        for kk in range(ncol // LANES):
            a = projg[xx * nc, :, kk * LANES : (kk + 1) * LANES].astype(F32)
            b = projg[xx * nc + 1, :, kk * LANES : (kk + 1) * LANES].astype(F32)
            pair = (
                jnp.where(left_half, a, pltpu.roll(b, wrows, 1)),
                jnp.where(left_half, pltpu.roll(a, wrows, 1), b),
            )
            for side in range(2):
                col = ((xx * nz + 2 * kk + side) * nc) * wrows
                base = resg[:, :, col : col + LANES].astype(F32).reshape(nrow, LANES)
                value = base + pair[side]
                hid[:, col : col + LANES] = value
                squares = squares + value * value
    inverse = lax.rsqrt(jnp.sum(squares, axis=1, keepdims=True) * (1.0 / width) + 1e-06)
    cstep = min(width, 512)
    for b in range(width // cstep):
        cs = slice(b * cstep, (b + 1) * cstep)
        values = (hid[:, cs] * inverse * gain_ref[:, cs].astype(F32)).astype(BF16)
        picked = dot(pick, values).astype(BF16)
        xs[t, 0, :, cs] = picked[:chunk]
        for i in range(1, nz):
            sel[i, :, cs] = picked[i * chunk : (i + 1) * chunk]
    for i in range(1, nz):
        send(sel.at[i], xs.at[t, i], sel_ss.at[i], sel_rs.at[i], z_peer(rel(i)))

    def forward(i):
        if i > 0:
            arrive(xs.at[t, i], sel_ss.at[i], sel_rs.at[i])
        for d in range(1, nt):
            send(xs.at[t, i], xs.at[t, i], xs_ss.at[i, d], xs_rs.at[i, d], t_peer(d))

    per = 2
    forward(0)
    forward(1)

    for d in range(1, nt):
        arrive(info.at[t_index(-d + nt)], infoy_ss.at[d], infoy_rs.at[d])
    places = nz * nt * chunk
    block = nt * chunk
    slot_no = lax.broadcasted_iota(jnp.int32, (LANES, places), 1)
    at_z = (z + rel(slot_no // block) + nz) % nz
    expert = (x * nz + at_z) * nc + c
    spread = (lax.broadcasted_iota(jnp.int32, (LANES, places), 0) == expert).astype(BF16)
    for tt in range(nt):
        code = info[tt, :, 0].reshape(nrow, LANES).astype(BF16)
        weight = info[tt, :, 1].reshape(nrow, LANES).astype(BF16)
        seen = dot(code, spread)
        given = dot(weight, spread)
        slot_no = lax.broadcasted_iota(jnp.int32, (nrow, places), 1)
        row_no = lax.broadcasted_iota(jnp.int32, (nrow, places), 0) + tt * nrow
        fits = (seen == (slot_no % CAP).astype(F32)) & (row_no // rows == (slot_no % block) // CAP)
        comb[tt * nrow : (tt + 1) * nrow, :] = jnp.where(fits, given, 0.0).astype(BF16)

    g_load.wait()
    u_load.wait()
    d_load.wait()
    for d in range(1, nt):
        arrive(dwg.at[t_index(-d + nt)], dw_ss.at[d], dw_rs.at[d])

    prow = nt * per * chunk

    def first(p):
        for i in range(per * p, per * p + per):
            for d in range(1, nt):
                arrive(xs.at[t_index(-d + nt), i], xs_ss.at[i, d], xs_rs.at[i, d])
        slots = xs[:, per * p : per * p + per].reshape(prow, width)
        both = dot(slots, gu[...])
        gate, up = both[:, :hidden_units], both[:, hidden_units:]
        act = (gate / (1.0 + jnp.exp(-gate)) * up).astype(BF16)
        actg[t, p] = act
        for d in range(1, nt):
            send(actg.at[t, p], actg.at[t, p], act_ss.at[p, d], act_rs.at[p, d], t_peer(d))

    def second(p):
        for d in range(1, nt):
            arrive(actg.at[t_index(-d + nt), p], act_ss.at[p, d], act_rs.at[p, d])
        total = dot(actg[0, p], dwg[0])
        for tt in range(1, nt):
            total = total + dot(actg[tt, p], dwg[tt])
        total = total.astype(BF16).reshape(nt, per, chunk, quarter)
        for k in range(per):
            i = per * p + k
            value = total[:, k].reshape(nt * chunk, quarter)
            if i == 0:
                ret_recv[0] = value
            else:
                ret_send[i] = value
                send(ret_send.at[i], ret_recv.at[i], ret_ss.at[i], ret_rs.at[i], z_peer(-rel(i)))

    for p in range(nz // per):
        if p < nz // per - 1:
            for k in range(per):
                forward(per * (p + 1) + k)
        first(p)
        if p > 0:
            second(p - 1)
    second(nz // per - 1)

    for i in range(1, nz):
        arrive(ret_recv.at[i], ret_ss.at[i], ret_rs.at[i])
    back = ret_recv[...].reshape(places, quarter)
    for tt in range(nt):
        part = dot(comb[tt * nrow : (tt + 1) * nrow, :], back).reshape(ns, rows, quarter)
        for ss in range(ns):
            fin_send[ss, tt * rows : (tt + 1) * rows, :] = part[ss].astype(BF16)
    for d in range(1, ns):
        send(fin_send.at[s_index(d)], fin_recv.at[s], fin_ss.at[d], fin_rs.at[d], s_peer(d))
    total = fin_send[s].astype(F32)
    for d in range(1, ns):
        p = s_index(-d + ns)
        arrive(fin_recv.at[p], fin_ss.at[d], fin_rs.at[d])
        total = total + fin_recv[p].astype(F32)
    for tt in range(nt):
        fy_send[tt] = total[tt * rows : (tt + 1) * rows]
    for d in range(1, nt):
        send(fy_send.at[t_index(d)], fy_recv.at[t], fy_ss.at[d], fy_rs.at[d], t_peer(d))
    fy_recv[t] = fy_send[t]
    for d in range(1, nt):
        arrive(fy_recv.at[t_index(-d + nt)], fy_ss.at[d], fy_rs.at[d])
    own = pl.ds(pl.multiple_of(s * rows, rows), rows)
    for tt in range(nt):
        cs = slice(tt * quarter, (tt + 1) * quarter)
        out_ref[:, cs] = (hid[own, cs] + fy_recv[tt]).astype(BF16)
    for copy in pending:
        copy.wait_send()


def on_device(
    nt,
    queries,
    cache_keys,
    cache_values,
    new_keys,
    new_values,
    lengths,
    out_weight,
    residual,
    norm_gain,
    routes,
    route_weights,
    gate_weight,
    up_weight,
    down_weight,
):
    nx, nz, nc = EP_SHAPE
    ns = nx * nc
    group_rows, heads, head_size = queries.shape
    context = cache_keys.shape[2]
    flat = heads * head_size
    rows, width = residual.shape[1:]
    wcols = out_weight.shape[1]
    units = gate_weight.shape[2]
    quarter = width // nt
    chunk = ns * CAP
    nrow = ns * rows
    ncol = nz * wcols
    dma = pltpu.SemaphoreType.DMA
    vmem = pltpu.VMEM
    scratch = [
        vmem((group_rows, heads, head_size), BF16),
        vmem((group_rows, context, head_size), BF16),
        vmem((group_rows, context, head_size), BF16),
        vmem((group_rows, heads, head_size), F32),
        vmem((2, group_rows, 1, head_size), F32),
        vmem((nz, wcols, flat), BF16),
        vmem((ns, group_rows, flat), BF16),
        vmem((nt, nrow, ncol), BF16),
        vmem((nt, nrow, ncol), BF16),
        vmem((ns, nrow, ncol), BF16),
        vmem((ns, rows, width), BF16),
        vmem((nrow, width), F32),
        vmem((nt, ns, 2, rows, LANES), F32),
        vmem((nt * nrow, nz * nt * chunk), BF16),
        vmem((nz, chunk, width), BF16),
        vmem((nt, nz, chunk, width), BF16),
        vmem((width, 2 * units), BF16),
        vmem((nt, units, quarter), BF16),
        vmem((nt, nz // 2, nt * 2 * chunk, units), BF16),
        vmem((nz, nt * chunk, quarter), BF16),
        vmem((nz, nt * chunk, quarter), BF16),
        vmem((ns, group_rows, quarter), BF16),
        vmem((ns, group_rows, quarter), BF16),
        vmem((nt, rows, quarter), F32),
        vmem((nt, rows, quarter), F32),
        dma((8,)),
        dma((2, max(nz // 2, 1))),
        dma((2, max(nz // 2, 1))),
        dma((ns,)),
        dma((ns,)),
        dma((ns,)),
        dma((ns,)),
        dma((ns,)),
        dma((ns,)),
        dma((nt,)),
        dma((nt,)),
        dma((nt,)),
        dma((nt,)),
        dma((nt,)),
        dma((nt,)),
        dma((ns,)),
        dma((ns,)),
        dma((nz,)),
        dma((nz,)),
        dma((nz, nt)),
        dma((nz, nt)),
        dma((nz // 2, nt)),
        dma((nz // 2, nt)),
        dma((nz,)),
        dma((nz,)),
        dma((ns,)),
        dma((ns,)),
        dma((nt,)),
        dma((nt,)),
    ]
    in_vmem = pl.BlockSpec(memory_space=pltpu.VMEM)
    anywhere = pl.BlockSpec(memory_space=pl.ANY)
    out = pl.pallas_call(
        functools.partial(kernel, (nx, nz, nc, nt)),
        out_shape=jax.ShapeDtypeStruct((rows, width), BF16),
        in_specs=[pl.BlockSpec(memory_space=pltpu.SMEM)] + [in_vmem] * 5 + [anywhere] * 8,
        out_specs=in_vmem,
        scratch_shapes=scratch,
        compiler_params=pltpu.CompilerParams(
            collective_id=0, has_side_effects=True, vmem_limit_bytes=VMEM_LIMIT
        ),
        name="layer",
    )(
        lengths,
        new_keys[:, 0],
        new_values[:, 0],
        norm_gain[None],
        routes[0],
        route_weights[0],
        queries,
        cache_keys[:, 0],
        cache_values[:, 0],
        out_weight.T,
        residual[0],
        gate_weight[0],
        up_weight[0],
        down_weight[0],
    )
    return out[None]


def solution(mesh):
    placed = (
        P("ep", "tp", None),
        P("ep", "tp", None, None),
        P("ep", "tp", None, None),
        P("ep", "tp", None),
        P("ep", "tp", None),
        P("ep"),
        P("tp", "ep"),
        P("ep", "tp", None),
        P(),
        P("ep", "tp", None),
        P("ep", "tp", None),
        P("ep", None, "tp"),
        P("ep", None, "tp"),
        P("ep", "tp", None),
    )
    return jax.shard_map(
        functools.partial(on_device, mesh.shape["tp"]),
        mesh=mesh,
        in_specs=placed,
        out_specs=P("ep", "tp", None),
        check_vma=False,
    )
```

time: 532 us -> 165 us (0.31)
  waiting for transfers between devices: 228 us -> 0 us
  blocking collectives: 209 us -> 0 us
  Pallas kernels: 0 us -> 162 us
  matrix products: 31.3 us -> 0 us
  local copies, waits for them, and re-layouts: 33.8 us -> 2.78 us
  between operations: 13.3 us -> 0.01 us
  starting transfers between devices: 12.6 us -> 0 us
    all_to_all x2 -> x0, blocking collectives: 209 us -> none  [the longest x1 107 us: on_device(): lax.all_to_all(stacked, 'ep', split_axis=0, concat_axis=0, tiled=True)]
    pallas_call x0 -> x1, Pallas kernels: none -> 162 us  [on_device(): pl.pallas_call(functools.partial(kernel, (nx, nz, nc, nt)), out_shape=jax...]
    all_gather x2 -> x0, waiting for transfers between devices: 132 us -> none  [the longest x1 87.3 us: on_device(): lax.all_gather(attn_flat, 'ep', axis=0, tiled=True)]
    reduce_scatter x1 -> x0, waiting for transfers between devices: 44.4 us -> none  [on_device(): lax.psum_scatter(returned.astype(jnp.float32).astype(jnp.bfloat16), 'tp',...]
    unnamed x5 -> x0, waiting for transfers between devices: 42.1 us -> none
    dot_general x8 -> x0, matrix products: 31.3 us -> none  [the longest x1 9.76 us: run_expert(): part_sum = jnp.dot(act, down_w, preferred_element_type=jnp.float32)]
    reshape x2 -> x0, local copies, waits for them, and re-layouts: 14.8 us -> none  [the longest x1 7.59 us: on_device(): run_expert(arrived.reshape(-1, model_width), gate_w, up_w, down_w)]
    all_to_all x1 -> x0, starting transfers between devices: 12.5 us -> none  [on_device(): lax.all_to_all(mine, 'ep', split_axis=0, concat_axis=3, tiled=True)]
  transfers between devices with their start and end apart: 5 -> 0, of which waited for: 5 -> 0; matrix products, arithmetic and copies ran while one was open for 0% -> 0% of each run, Pallas kernels for 0% -> 0%
where the time goes in v1:
time: 165 us
  Pallas kernels  162 us (98%)
  local copies, waits for them, and re-layouts  2.78 us (2%)
    pallas_call x1, Pallas kernels, on_device(): pl.pallas_call(functools.partial(kernel, (nx, nz, nc, nt)), out_shape=jax...  162 us

profile of v1, /device:TPU:1, one launch (start us, length us, event | category | flops | bytes accessed | tf_op | source)
XLA Modules:
  0.0 164.6 jit_solution(10998108768114140491)
XLA Ops:
  0.0 1.3 broadcast_in_dim.6.gain_ref
  1.3 161.8 %layer.1 = bf16[8,4096]{1,0:T(8,128)(2,1)} custom-call(s32[32]{0:T(128)} %lengths_ref.1, bf16[32,128]{1,0:T(8,128)(2,1)} %bitcast.20, bf16[32,128]{1,0:T(8,128)(2,1)} %bitcast.21, bf16[1,4096]{1,0:T(2,128)(2,1)} %broadcast_in_dim.6.gain_ref, s32[8,8]{1,0:T(8,128)} %bitcast.22, f32[8,8]{1,0:T(8,128)} %bitcast.23, bf16[32,16,128]{2,1,0:T(8,128)(2,1)} %q_hbm.1, ...), custom_call_target="tpu_custom_call" | custom-call | tf_op jit(solution)/shard_map/layer/pallas_call | solution.py:533
  163.2 1.5 copy.16

commit v2 on v1

v2 whole, which is shorter than its diff:
```python
import functools

import jax
import jax.numpy as jnp
from jax import lax
from jax.experimental import pallas as pl
from jax.experimental.pallas import tpu as pltpu
from jax.sharding import PartitionSpec as P

MESH = pl.DeviceIdType.MESH
BF16 = jnp.bfloat16
F32 = jnp.float32
EP_SHAPE = (4, 8, 2)
LANES = 128
CAP = 2
VMEM_LIMIT = 60 * 1024 * 1024


def dot(a, b):
    return jnp.dot(a, b, preferred_element_type=F32)


def dot_nt(a, b):
    return lax.dot_general(a, b, (((1,), (1,)), ((), ())), preferred_element_type=F32)


def offsets(nz):
    return {8: (0, -1, 2, -3, 4, 3, -2, 1), 4: (0, 2, 1, -1), 2: (0, 1)}[nz]


def offset_of(index, nz):
    value = jnp.zeros_like(index)
    for i, d in enumerate(offsets(nz)):
        value = jnp.where(index == i, d, value)
    return value


def kernel(
    dims,
    lengths_ref,
    nk_hbm,
    nv_hbm,
    gain_hbm,
    routes_hbm,
    shares_hbm,
    q_hbm,
    k_hbm,
    v_hbm,
    wt_hbm,
    res_hbm,
    gate_hbm,
    up_hbm,
    down_hbm,
    out_ref,
    nk_ref,
    nv_ref,
    gain_ref,
    routes_ref,
    shares_ref,
    q_buf,
    k_buf,
    v_buf,
    mixed_buf,
    wg,
    xg,
    rs_send,
    rs_recv,
    projg,
    resg,
    hid,
    info,
    comb,
    sel,
    xs,
    gu,
    dwg,
    actg,
    ret_send,
    ret_recv,
    early_sum,
    fin_send,
    fin_pair,
    fin_sum,
    fin_recv,
    fy_send,
    fy_recv,
    load_sem,
    ring_ss,
    ring_rs,
    x_ss,
    x_rs,
    res_ss,
    res_rs,
    info_ss,
    info_rs,
    infoy_ss,
    infoy_rs,
    dw_ss,
    dw_rs,
    rs_ss,
    rs_rs,
    proj_ss,
    proj_rs,
    sel_ss,
    sel_rs,
    xs_ss,
    xs_rs,
    far_ss,
    far_rs,
    act_ss,
    act_rs,
    ret_ss,
    ret_rs,
    fin_ss,
    fin_rs,
    fy_ss,
    fy_rs,
):
    nx, nz, nc, nt = dims
    ns = nx * nc
    rows = res_hbm.shape[0]
    width = res_hbm.shape[1]
    quarter = width // nt
    group_rows = nt * rows
    heads, head_size = q_buf.shape[1], q_buf.shape[2]
    context = k_hbm.shape[1]
    hidden_units = gate_hbm.shape[1]
    chunk = ns * CAP

    ep = lax.axis_index("ep")
    t = lax.axis_index("tp")
    x = ep // (nz * nc)
    z = (ep // nc) % nz
    c = ep % nc
    s = x * nc + c

    def z_peer(d):
        return {"ep": (x * nz + (z + d + nz) % nz) * nc + c, "tp": t}

    sibling = {"ep": (x * nz + z) * nc + 1 - c, "tp": t}

    def x_index(d):
        return (x + d) % nx

    def x_peer(d):
        return {"ep": (x_index(d) * nz + z) * nc + c, "tp": t}

    def t_index(d):
        return (t + d) % nt

    def t_peer(d):
        return {"ep": ep, "tp": t_index(d)}

    pending = []

    def describe(src, dst, sems, at, peer):
        return pltpu.make_async_remote_copy(
            src_ref=src,
            dst_ref=dst,
            send_sem=sems[0].at[at],
            recv_sem=sems[1].at[at],
            device_id=peer,
            device_id_type=MESH,
        )

    def send(src, dst, sems, at, peer):
        copy = describe(src, dst, sems, at, peer)
        copy.start()
        pending.append(copy)

    def arrive(dst, sems, at):
        describe(dst, dst, sems, at, t_peer(1)).wait_recv()

    def spread_start(view, sems, own=None, pre=()):
        own = view(s) if own is None else own
        for d in range(1, nx):
            send(own, view(s), sems, pre + (0, d), x_peer(d))
        send(own, view(s), sems, pre + (1, 0), sibling)

    def spread_relay(view, sems, pre=()):
        for d in range(1, nx):
            block = view(x_index(nx - d) * nc + c)
            arrive(block, sems, pre + (0, d))
            send(block, block, sems, pre + (1, d), sibling)

    def spread_end(view, sems, pre=()):
        for d in range(nx):
            arrive(view(x_index(nx - d) * nc + 1 - c), sems, pre + (1, d))

    barrier = pltpu.get_barrier_semaphore()
    partners = (
        [z_peer(d) for d in range(1, nz)]
        + [x_peer(d) for d in range(1, nx)]
        + [sibling]
        + [t_peer(d) for d in range(1, nt)]
    )
    for peer in partners:
        pl.semaphore_signal(barrier, inc=1, device_id=peer, device_id_type=MESH)

    def load(src, dst, n):
        copy = pltpu.make_async_copy(src, dst, load_sem.at[n])
        copy.start()
        return copy

    q_load = load(q_hbm, q_buf, 0)
    k_load = load(k_hbm, k_buf.at[:, pl.ds(0, context)], 1)
    v_load = load(v_hbm, v_buf.at[:, pl.ds(0, context)], 2)
    small_loads = [
        load(src, dst, 8 + n)
        for n, (src, dst) in enumerate(
            (
                (nk_hbm, nk_ref),
                (nv_hbm, nv_ref),
                (gain_hbm, gain_ref),
                (routes_hbm, routes_ref),
                (shares_hbm, shares_ref),
            )
        )
    ]
    w_load = load(wt_hbm, wg.at[nz - 2], 3)
    r_load = load(res_hbm, resg.at[s], 4)

    lane = lax.broadcasted_iota(jnp.int32, (rows, LANES), 1)
    row = lax.broadcasted_iota(jnp.int32, (rows, LANES), 0)
    member = jnp.zeros((rows, LANES), F32)
    share = jnp.zeros((rows, LANES), F32)
    for n in (3, 4):
        small_loads[n].wait()
    routes = routes_ref[...]
    shares = shares_ref[...]
    for k in range(routes.shape[1]):
        hit = routes[:, k : k + 1] == lane
        member = jnp.where(hit, 1.0, member)
        share = share + jnp.where(hit, shares[:, k : k + 1], 0.0)
    rank = jnp.zeros((rows, LANES), F32)
    for j in range(rows - 1):
        rank = rank + jnp.where(row > j, member[j : j + 1, :], 0.0)
    info[t, s, 0] = jnp.where(member > 0.0, rank, -1.0)
    info[t, s, 1] = share

    pl.semaphore_wait(barrier, len(partners))

    half = nz // 2
    wrows = wt_hbm.shape[0]
    top, low = pl.ds(0, wrows // 2), pl.ds(wrows // 2, wrows // 2)

    pieces = (top, low)

    def ring_slot(side, j):
        return nz - 1 if j == half else 2 * (j - 1) + side

    def ring_send(j, k):
        for side, d in enumerate((1, -1)):
            if j == half and k != side:
                continue
            src = wt_hbm if j == 1 else wg.at[ring_slot(side, j - 1)]
            dst = wg.at[ring_slot(side, j), pieces[k]]
            send(src.at[pieces[k]], dst, (ring_ss, ring_rs), (side, j - 1, k), z_peer(d))

    def ring_wait(j, k):
        for side in range(2):
            if j == half and k != side:
                continue
            dst = wg.at[ring_slot(side, j), pieces[k]]
            arrive(dst, (ring_ss, ring_rs), (side, j - 1, k))

    events = [(j, k) for j in range(1, half) for k in range(2)]

    def ring_event():
        if events:
            j, k = events.pop(0)
            ring_wait(j, k)
            ring_send(j + 1, k)

    for k in range(2):
        ring_send(1, k)

    def info_of(p):
        return info.at[t, p]

    def res_of(p):
        return resg.at[p]

    def x_of(p):
        return xg.at[p]

    spread_start(info_of, (info_ss, info_rs))
    spread_start(res_of, (res_ss, res_rs), res_hbm)
    unit_cut = hidden_units * 3 // 4

    unit_parts = (pl.ds(0, unit_cut), pl.ds(unit_cut, hidden_units - unit_cut))

    def send_down(k):
        for d in range(1, nt):
            part = pl.ds(pl.multiple_of(t_index(d) * quarter, LANES), quarter)
            units = unit_parts[k]
            send(down_hbm.at[units, part], dwg.at[t, units], (dw_ss, dw_rs), (k, d), t_peer(d))

    send_down(0)

    tail = k_buf.shape[1] - context
    at_slot = lax.broadcasted_iota(jnp.int32, (group_rows, tail, head_size), 1) == 0
    for n in (0, 1, 2):
        small_loads[n].wait()
    for buf, fresh in ((k_buf, nk_ref), (v_buf, nv_ref)):
        value = jnp.where(at_slot, fresh[...].astype(F32)[:, None, :], 0.0)
        buf[:, context:, :] = value.astype(BF16)
    q_load.wait()
    k_load.wait()
    v_load.wait()
    g_load = load(gate_hbm, gu.at[:, pl.ds(0, hidden_units)], 5)
    u_load = load(up_hbm, gu.at[:, pl.ds(hidden_units, hidden_units)], 6)
    my_quarter = pl.ds(pl.multiple_of(t * quarter, LANES), quarter)
    d_load = load(down_hbm.at[:, my_quarter], dwg.at[t], 7)
    scale = head_size ** (-0.5)
    step_rows = 8

    def attend(g):
        slot = lax.broadcasted_iota(jnp.int32, (heads, context + tail), 1)
        rows_here = [g * step_rows + j for j in range(step_rows)]
        scores = [dot_nt(q_buf[r], k_buf[r]) for r in rows_here]
        probs = []
        for r, score in zip(rows_here, scores):
            valid = (slot < lengths_ref[r]) | (slot == context)
            score = jnp.where(valid, score * scale, -1e30)
            weight = jnp.exp(score - jnp.max(score, axis=1, keepdims=True))
            total = jnp.sum(weight, axis=1, keepdims=True)
            probs.append((weight * (1.0 / total)).astype(BF16))
        for r, prob in zip(rows_here, probs):
            mixed_buf[r] = dot(prob, v_buf[r])

    for g in range(group_rows // step_rows):
        attend(g)
        ring_event()
    for h in range(heads):
        xg[s, :, h * head_size : (h + 1) * head_size] = mixed_buf[:, h, :].astype(BF16)
    spread_start(x_of, (x_ss, x_rs))
    spread_relay(info_of, (info_ss, info_rs))
    spread_relay(res_of, (res_ss, res_rs))
    spread_end(info_of, (info_ss, info_rs))
    for d in range(1, nt):
        send(info.at[t], info.at[t], (infoy_ss, infoy_rs), (d,), t_peer(d))

    picks = nz * chunk
    slot_no = lax.broadcasted_iota(jnp.int32, (picks, LANES), 0)
    at_z = (z + offset_of(slot_no // chunk, nz) + nz) % nz
    expert = (x * nz + at_z) * nc + c
    spread = (lax.broadcasted_iota(jnp.int32, (picks, LANES), 1) == expert).astype(BF16)
    code = info[t, :, 0].reshape(ns * rows, LANES).astype(BF16)
    seen = dot_nt(spread, code)
    slot_no = lax.broadcasted_iota(jnp.int32, (picks, ns * rows), 0)
    row_no = lax.broadcasted_iota(jnp.int32, (picks, ns * rows), 1)
    pick = (
        (seen == (slot_no % CAP).astype(F32)) & (row_no // rows == (slot_no % chunk) // CAP)
    ).astype(BF16)

    while events:
        ring_event()
    spread_relay(x_of, (x_ss, x_rs))
    spread_end(x_of, (x_ss, x_rs))

    nrow = ns * rows
    ncol = half * wrows
    all_rows = xg[...].reshape(ns * group_rows, xg.shape[2])

    def project(q):
        cols = wg[q * half : (q + 1) * half].reshape(ncol, wg.shape[2])
        part = dot_nt(all_rows, cols).reshape(ns, nt, rows, ncol)
        for tt in range(nt):
            rs_send[q, tt] = part[:, tt].reshape(nrow, ncol).astype(BF16)
        for d in range(1, nt):
            send(rs_send.at[q, t_index(d)], rs_recv.at[q, t], (rs_ss, rs_rs), (q, d), t_peer(d))

    def proj_of(q):
        return lambda p: projg.at[q, p]

    def gather(q):
        total = rs_send[q, t].astype(F32)
        for d in range(1, nt):
            p = t_index(nt - d)
            arrive(rs_recv.at[q, p], (rs_ss, rs_rs), (q, d))
            total = total + rs_recv[q, p].astype(F32)
        projg[q, s] = total.astype(BF16)
        spread_start(proj_of(q), (proj_ss, proj_rs), pre=(q,))

    w_load.wait()
    project(0)
    ring_wait(half, 0)
    ring_wait(half, 1)
    project(1)
    gather(0)
    gather(1)
    send_down(1)
    spread_end(res_of, (res_ss, res_rs))
    r_load.wait()

    left_half = lax.broadcasted_iota(jnp.int32, (nrow, LANES), 1) < wrows
    squares = jnp.zeros((nrow, LANES), F32)
    npair = ncol // LANES
    for q in range(2):
        spread_relay(proj_of(q), (proj_ss, proj_rs), pre=(q,))
        spread_end(proj_of(q), (proj_ss, proj_rs), pre=(q,))
        for m in range(npair):
            j = q * npair + m + 1
            blocks = ((z - j + nz) % nz, (z + j) % nz) if j < half else (z, (z + half) % nz)
            lanes = slice(m * LANES, (m + 1) * LANES)
            for xx in range(nx):
                a = projg[q, xx * nc, :, lanes].astype(F32)
                b = projg[q, xx * nc + 1, :, lanes].astype(F32)
                pair = (
                    jnp.where(left_half, a, pltpu.roll(b, wrows, 1)),
                    jnp.where(left_half, pltpu.roll(a, wrows, 1), b),
                )
                for side in range(2):
                    col = pl.ds(pl.multiple_of((xx * nz + blocks[side]) * LANES, LANES), LANES)
                    base = resg[:, :, col].astype(F32).reshape(nrow, LANES)
                    value = base + pair[side]
                    hid[:, col] = value
                    squares = squares + value * value
    inverse = lax.rsqrt(jnp.sum(squares, axis=1, keepdims=True) * (1.0 / width) + 1e-06)
    cstep = min(width, 512)
    gain = gain_ref[...].astype(F32)
    for b in range(width // cstep):
        cs = slice(b * cstep, (b + 1) * cstep)
        values = []
        for j in range(b * cstep // LANES, (b + 1) * cstep // LANES):
            value = hid[:, j * LANES : (j + 1) * LANES] * inverse * gain[j : j + 1, :]
            values.append(value.astype(BF16))
        picked = dot(pick, jnp.concatenate(values, axis=1)).astype(BF16)
        xs[t, 0, :, cs] = picked[:chunk]
        for i in range(1, nz):
            sel[i, :, cs] = picked[i * chunk : (i + 1) * chunk]

    def send_chunk(i):
        if i < nz:
            send(sel.at[i], xs.at[t, i], (sel_ss, sel_rs), (i,), z_peer(offsets(nz)[i]))

    for i in (1, 2):
        send_chunk(i)

    def forward(i):
        if i > 0:
            arrive(xs.at[t, i], (sel_ss, sel_rs), (i,))
            send_chunk(i + 2)
        for d in (1, nt - 1):
            send(xs.at[t, i], xs.at[t, i], (xs_ss, xs_rs), (i, d), t_peer(d))

    def relay(i):
        for k, d in enumerate((1, nt - 1)):
            arrive(xs.at[t_index(nt - d), i], (xs_ss, xs_rs), (i, d))
            part = xs.at[t_index(nt - d), i, :, pl.ds(k * (width // 2), width // 2)]
            send(part, part, (far_ss, far_rs), (i, k), t_peer(d))

    def complete(i):
        for k in range(2):
            part = xs.at[t_index(nt // 2), i, :, pl.ds(k * (width // 2), width // 2)]
            arrive(part, (far_ss, far_rs), (i, k))

    per = 2
    pairs = nz // per
    for i in range(min(2 * per, nz)):
        forward(i)
    for i in range(per):
        relay(i)

    for d in range(1, nt):
        arrive(info.at[t_index(-d + nt)], (infoy_ss, infoy_rs), (d,))
    places = nz * nt * chunk
    block = nt * chunk
    slot_no = lax.broadcasted_iota(jnp.int32, (LANES, places), 1)
    at_z = (z + offset_of(slot_no // block, nz) + nz) % nz
    expert = (x * nz + at_z) * nc + c
    spread = (lax.broadcasted_iota(jnp.int32, (LANES, places), 0) == expert).astype(BF16)
    for tt in range(nt):
        code = info[tt, :, 0].reshape(nrow, LANES).astype(BF16)
        weight = info[tt, :, 1].reshape(nrow, LANES).astype(BF16)
        seen = dot(code, spread)
        given = dot(weight, spread)
        slot_no = lax.broadcasted_iota(jnp.int32, (nrow, places), 1)
        row_no = lax.broadcasted_iota(jnp.int32, (nrow, places), 0) + tt * nrow
        fits = (seen == (slot_no % CAP).astype(F32)) & (row_no // rows == (slot_no % block) // CAP)
        comb[tt * nrow : (tt + 1) * nrow, :] = jnp.where(fits, given, 0.0).astype(BF16)

    g_load.wait()
    u_load.wait()

    prow = nt * per * chunk

    def first(p):
        for i in range(per * p, per * p + per):
            complete(i)
        slots = xs[:, per * p : per * p + per].reshape(prow, width)
        both = dot(slots, gu[...])
        gate, up = both[:, :hidden_units], both[:, hidden_units:]
        act = (gate / (1.0 + jnp.exp(-gate)) * up).astype(BF16)
        actg[t, p] = act
        for d in range(1, nt):
            send(actg.at[t, p], actg.at[t, p], (act_ss, act_rs), (p, d), t_peer(d))

    def second(p):
        if p == 0:
            d_load.wait()
            for d in range(1, nt):
                for k in range(2):
                    units = unit_parts[k]
                    arrive(dwg.at[t_index(-d + nt), units], (dw_ss, dw_rs), (k, d))
        for d in range(1, nt):
            arrive(actg.at[t_index(-d + nt), p], (act_ss, act_rs), (p, d))
        total = dot(actg[0, p], dwg[0])
        for tt in range(1, nt):
            total = total + dot(actg[tt, p], dwg[tt])
        total = total.astype(BF16).reshape(nt, per, chunk, quarter)
        for k in range(per):
            i = per * p + k
            value = total[:, k].reshape(nt * chunk, quarter)
            if i == 0:
                ret_recv[0] = value
            else:
                ret_send[i] = value
                send(ret_send.at[i], ret_recv.at[i], (ret_ss, ret_rs), (i), z_peer(-offsets(nz)[i]))

    for p in range(pairs):
        for k in range(per):
            if p < pairs - 2:
                forward(per * (p + 2) + k)
            if p < pairs - 1:
                relay(per * (p + 1) + k)
        first(p)
        if p > 0:
            second(p - 1)
    second(pairs - 1)

    early = nz - per
    for i in range(1, early):
        arrive(ret_recv.at[i], (ret_ss, ret_rs), (i,))
    back = ret_recv[:early].reshape(early * block, quarter)
    early_sum[...] = dot(comb[:, : early * block], back)
    for i in range(early, nz):
        arrive(ret_recv.at[i], (ret_ss, ret_rs), (i,))
    back = ret_recv[early:].reshape(per * block, quarter)
    for tt in range(nt):
        these = slice(tt * nrow, (tt + 1) * nrow)
        part = dot(comb[these, early * block :], back) + early_sum[these, :]
        part = part.reshape(nx, nc, rows, quarter).astype(BF16)
        for xx in range(nx):
            for cc in range(nc):
                fin_send[cc, xx, tt * rows : (tt + 1) * rows, :] = part[xx, cc]
    send(fin_send.at[1 - c], fin_pair, (fin_ss, fin_rs), (0,), sibling)
    arrive(fin_pair, (fin_ss, fin_rs), (0,))
    for d in range(1, nx):
        p = x_index(d)
        fin_sum[p] = (fin_send[c, p].astype(F32) + fin_pair[p].astype(F32)).astype(BF16)
        send(fin_sum.at[p], fin_recv.at[x], (fin_ss, fin_rs), (d,), x_peer(d))
    total = fin_send[c, x].astype(F32) + fin_pair[x].astype(F32)
    for d in range(1, nx):
        p = x_index(nx - d)
        arrive(fin_recv.at[p], (fin_ss, fin_rs), (d,))
        total = total + fin_recv[p].astype(F32)
    for tt in range(nt):
        fy_send[tt] = total[tt * rows : (tt + 1) * rows]
    for d in range(1, nt):
        send(fy_send.at[t_index(d)], fy_recv.at[t], (fy_ss, fy_rs), (d,), t_peer(d))
    fy_recv[t] = fy_send[t]
    for d in range(1, nt):
        arrive(fy_recv.at[t_index(-d + nt)], (fy_ss, fy_rs), (d,))
    own = pl.ds(pl.multiple_of(s * rows, rows), rows)
    for tt in range(nt):
        cs = slice(tt * quarter, (tt + 1) * quarter)
        out_ref[:, cs] = (hid[own, cs] + fy_recv[tt]).astype(BF16)
    for copy in pending:
        copy.wait_send()


def on_device(
    nt,
    queries,
    cache_keys,
    cache_values,
    new_keys,
    new_values,
    lengths,
    out_weight,
    residual,
    norm_gain,
    routes,
    route_weights,
    gate_weight,
    up_weight,
    down_weight,
):
    nx, nz, nc = EP_SHAPE
    ns = nx * nc
    group_rows, heads, head_size = queries.shape
    context = cache_keys.shape[2]
    flat = heads * head_size
    rows, width = residual.shape[1:]
    wcols = out_weight.shape[1]
    units = gate_weight.shape[2]
    quarter = width // nt
    chunk = ns * CAP
    nrow = ns * rows
    ncol = nz // 2 * wcols
    dma = pltpu.SemaphoreType.DMA
    vmem = pltpu.VMEM
    scratch = [
        vmem((group_rows, head_size), BF16),
        vmem((group_rows, head_size), BF16),
        vmem((width // LANES, LANES), BF16),
        vmem(routes.shape[1:], jnp.int32),
        vmem(routes.shape[1:], F32),
        vmem((group_rows, heads, head_size), BF16),
        vmem((group_rows, context + 16, head_size), BF16),
        vmem((group_rows, context + 16, head_size), BF16),
        vmem((group_rows, heads, head_size), F32),
        vmem((nz, wcols, flat), BF16),
        vmem((ns, group_rows, flat), BF16),
        vmem((2, nt, nrow, ncol), BF16),
        vmem((2, nt, nrow, ncol), BF16),
        vmem((2, ns, nrow, ncol), BF16),
        vmem((ns, rows, width), BF16),
        vmem((nrow, width), F32),
        vmem((nt, ns, 2, rows, LANES), F32),
        vmem((nt * nrow, nz * nt * chunk), BF16),
        vmem((nz, chunk, width), BF16),
        vmem((nt, nz, chunk, width), BF16),
        vmem((width, 2 * units), BF16),
        vmem((nt, units, quarter), BF16),
        vmem((nt, nz // 2, nt * 2 * chunk, units), BF16),
        vmem((nz, nt * chunk, quarter), BF16),
        vmem((nz, nt * chunk, quarter), BF16),
        vmem((nt * nrow, quarter), F32),
        vmem((nc, nx, group_rows, quarter), BF16),
        vmem((nx, group_rows, quarter), BF16),
        vmem((nx, group_rows, quarter), BF16),
        vmem((nx, group_rows, quarter), BF16),
        vmem((nt, rows, quarter), F32),
        vmem((nt, rows, quarter), F32),
        dma((13,)),
    ]
    for shape in (
        (2, nz // 2, 2),
        (2, nx),
        (2, nx),
        (2, nx),
        (nt,),
        (2, nt),
        (2, nt),
        (2, 2, nx),
        (nz,),
        (nz, nt),
        (nz, 2),
        (nz // 2, nt),
        (nz,),
        (nx,),
        (nt,),
    ):
        scratch += [dma(shape), dma(shape)]
    in_vmem = pl.BlockSpec(memory_space=pltpu.VMEM)
    anywhere = pl.BlockSpec(memory_space=pl.ANY)
    out = pl.pallas_call(
        functools.partial(kernel, (nx, nz, nc, nt)),
        out_shape=jax.ShapeDtypeStruct((rows, width), BF16),
        in_specs=[pl.BlockSpec(memory_space=pltpu.SMEM)] + [anywhere] * 13,
        out_specs=in_vmem,
        scratch_shapes=scratch,
        compiler_params=pltpu.CompilerParams(
            collective_id=0, has_side_effects=True, vmem_limit_bytes=VMEM_LIMIT
        ),
        name="layer",
    )(
        lengths,
        new_keys[:, 0],
        new_values[:, 0],
        norm_gain.reshape(width // LANES, LANES),
        routes[0],
        route_weights[0],
        queries,
        cache_keys[:, 0],
        cache_values[:, 0],
        out_weight.T,
        residual[0],
        gate_weight[0],
        up_weight[0],
        down_weight[0],
    )
    return out[None]


def solution(mesh):
    placed = (
        P("ep", "tp", None),
        P("ep", "tp", None, None),
        P("ep", "tp", None, None),
        P("ep", "tp", None),
        P("ep", "tp", None),
        P("ep"),
        P("tp", "ep"),
        P("ep", "tp", None),
        P(),
        P("ep", "tp", None),
        P("ep", "tp", None),
        P("ep", None, "tp"),
        P("ep", None, "tp"),
        P("ep", "tp", None),
    )
    return jax.shard_map(
        functools.partial(on_device, mesh.shape["tp"]),
        mesh=mesh,
        in_specs=placed,
        out_specs=P("ep", "tp", None),
        check_vma=False,
    )
```

time: 165 us -> 141 us (0.85)
  Pallas kernels: 162 us -> 139 us
    pallas_call x1, Pallas kernels: 162 us -> 139 us  [on_device(): pl.pallas_call(functools.partial(kernel, (nx, nz, nc, nt)), out_shape=jax...]
where the time goes in v2:
time: 141 us
  Pallas kernels  139 us (99%)
  local copies, waits for them, and re-layouts  1.47 us (1%)
    pallas_call x1, Pallas kernels, on_device(): pl.pallas_call(functools.partial(kernel, (nx, nz, nc, nt)), out_shape=jax...  139 us

profile of v2, /device:TPU:1, one launch (start us, length us, event | category | flops | bytes accessed | tf_op | source)
XLA Modules:
  0.0 140.7 jit_solution(17240475188197354376)
XLA Ops:
  0.0 139.2 %layer.1 = bf16[8,4096]{1,0:T(8,128)(2,1)} custom-call(s32[32]{0:T(128)} %lengths_ref.1, bf16[32,128]{1,0:T(8,128)(2,1)} %bitcast.21, bf16[32,128]{1,0:T(8,128)(2,1)} %bitcast.22, bf16[32,128]{1,0:T(8,128)(2,1)} %bitcast.23, s32[8,8]{1,0:T(8,128)} %bitcast.24, f32[8,8]{1,0:T(8,128)} %bitcast.25, bf16[32,16,128]{2,1,0:T(8,128)(2,1)} %q_hbm.1, ...), custom_call_target="tpu_custom_call" | custom-call | tf_op jit(solution)/shard_map/layer/pallas_call | solution.py:660
  139.2 1.5 %copy.16 = bf16[1,8,4096]{2,1,0:T(8,128)(2,1)} copy(bf16[1,8,4096]{2,1,0:T(8,128)(2,1)} %bitcast.18) | data formatting | bytes 131072

commit v3 on v2

--- a/solution.py
+++ b/solution.py
@@ -25,7 +25,7 @@
 
 
 def offsets(nz):
-    return {8: (0, -1, 2, -3, 4, 3, -2, 1), 4: (0, 2, 1, -1), 2: (0, 1)}[nz]
+    return {8: (-1, 2, -3, 4, 3, -2, 1, 0), 4: (-1, 2, 1, 0)}[nz]
 
 
 def offset_of(index, nz):
@@ -109,6 +109,8 @@
     far_rs,
     act_ss,
     act_rs,
+    afar_ss,
+    afar_rs,
     ret_ss,
     ret_rs,
     fin_ss,
@@ -427,19 +429,19 @@
             value = hid[:, j * LANES : (j + 1) * LANES] * inverse * gain[j : j + 1, :]
             values.append(value.astype(BF16))
         picked = dot(pick, jnp.concatenate(values, axis=1)).astype(BF16)
-        xs[t, 0, :, cs] = picked[:chunk]
-        for i in range(1, nz):
+        xs[t, nz - 1, :, cs] = picked[(nz - 1) * chunk :]
+        for i in range(nz - 1):
             sel[i, :, cs] = picked[i * chunk : (i + 1) * chunk]
 
     def send_chunk(i):
-        if i < nz:
+        if i < nz - 1:
             send(sel.at[i], xs.at[t, i], (sel_ss, sel_rs), (i,), z_peer(offsets(nz)[i]))
 
-    for i in (1, 2):
+    for i in (0, 1):
         send_chunk(i)
 
     def forward(i):
-        if i > 0:
+        if i < nz - 1:
             arrive(xs.at[t, i], (sel_ss, sel_rs), (i,))
             send_chunk(i + 2)
         for d in (1, nt - 1):
@@ -457,11 +459,14 @@
             arrive(part, (far_ss, far_rs), (i, k))
 
     per = 2
-    pairs = nz // per
-    for i in range(min(2 * per, nz)):
-        forward(i)
-    for i in range(per):
-        relay(i)
+    groups = [range(k, k + per) for k in range(0, nz - per, per)]
+    groups += [range(k, k + 1) for k in range(nz - per, nz)]
+
+    forward(nz - 1)
+    forward(0)
+    relay(nz - 1)
+    forward(1)
+    relay(0)
 
     for d in range(1, nt):
         arrive(info.at[t_index(-d + nt)], (infoy_ss, infoy_rs), (d,))
@@ -484,58 +489,83 @@
     g_load.wait()
     u_load.wait()
 
-    prow = nt * per * chunk
-
     def first(p):
-        for i in range(per * p, per * p + per):
+        chunks = groups[p]
+        count = len(chunks)
+        these = pl.ds(chunks[0], count)
+        for i in chunks:
             complete(i)
-        slots = xs[:, per * p : per * p + per].reshape(prow, width)
+        slots = xs[:, chunks[0] : chunks[-1] + 1].reshape(nt * count * chunk, width)
         both = dot(slots, gu[...])
         gate, up = both[:, :hidden_units], both[:, hidden_units:]
-        act = (gate / (1.0 + jnp.exp(-gate)) * up).astype(BF16)
-        actg[t, p] = act
-        for d in range(1, nt):
-            send(actg.at[t, p], actg.at[t, p], (act_ss, act_rs), (p, d), t_peer(d))
+        act = (gate / (1.0 + jnp.exp(-gate)) * up).reshape(nt, count, chunk, hidden_units)
+        for k in range(count):
+            actg[t, chunks[k]] = act[:, k].reshape(block, hidden_units).astype(BF16)
+        part = actg.at[t, these]
+        for d in (1, nt - 1) if count > 1 else range(1, nt):
+            send(part, part, (act_ss, act_rs), (p, d), t_peer(d))
+
+    def relay_act(p):
+        for k, d in enumerate((1, nt - 1)):
+            src = t_index(nt - d)
+            arrive(actg.at[src, pl.ds(groups[p][0], per)], (act_ss, act_rs), (p, d))
+            part = actg.at[src, groups[p][k]]
+            send(part, part, (afar_ss, afar_rs), (p, k), t_peer(d))
 
     def second(p):
+        chunks = groups[p]
+        count = len(chunks)
         if p == 0:
             d_load.wait()
             for d in range(1, nt):
                 for k in range(2):
                     units = unit_parts[k]
                     arrive(dwg.at[t_index(-d + nt), units], (dw_ss, dw_rs), (k, d))
-        for d in range(1, nt):
-            arrive(actg.at[t_index(-d + nt), p], (act_ss, act_rs), (p, d))
-        total = dot(actg[0, p], dwg[0])
-        for tt in range(1, nt):
-            total = total + dot(actg[tt, p], dwg[tt])
-        total = total.astype(BF16).reshape(nt, per, chunk, quarter)
-        for k in range(per):
-            i = per * p + k
-            value = total[:, k].reshape(nt * chunk, quarter)
-            if i == 0:
-                ret_recv[0] = value
+        if count > 1:
+            for k in range(per):
+                arrive(actg.at[t_index(nt // 2), chunks[k]], (afar_ss, afar_rs), (p, k))
+        else:
+            for d in range(1, nt):
+                arrive(actg.at[t_index(nt - d), pl.ds(chunks[0], 1)], (act_ss, act_rs), (p, d))
+        total = jnp.zeros((count * block, quarter), F32)
+        for tt in range(nt):
+            part = actg[tt, chunks[0] : chunks[-1] + 1].reshape(count * block, hidden_units)
+            total = total + dot(part, dwg[tt])
+        for k, i in enumerate(chunks):
+            value = total[k * block : (k + 1) * block].astype(BF16)
+            if i == nz - 1:
+                ret_recv[i] = value
             else:
                 ret_send[i] = value
-                send(ret_send.at[i], ret_recv.at[i], (ret_ss, ret_rs), (i), z_peer(-offsets(nz)[i]))
-
-    for p in range(pairs):
-        for k in range(per):
-            if p < pairs - 2:
-                forward(per * (p + 2) + k)
-            if p < pairs - 1:
-                relay(per * (p + 1) + k)
+                send(
+                    ret_send.at[i],
+                    ret_recv.at[i],
+                    (ret_ss, ret_rs),
+                    (i,),
+                    z_peer(-offsets(nz)[i]),
+                )
+
+    last = len(groups) - 1
+    relay(1)
+    forward(2)
+    first(0)
+    for p in range(1, last + 1):
+        for i in range(per * p, min(per * p + per, nz - 1)):
+            if i + 1 < nz - 1:
+                forward(i + 1)
+            relay(i)
+        if len(groups[p - 1]) > 1:
+            relay_act(p - 1)
         first(p)
-        if p > 0:
-            second(p - 1)
-    second(pairs - 1)
+        second(p - 1)
 
     early = nz - per
-    for i in range(1, early):
+    for i in range(early):
         arrive(ret_recv.at[i], (ret_ss, ret_rs), (i,))
     back = ret_recv[:early].reshape(early * block, quarter)
     early_sum[...] = dot(comb[:, : early * block], back)
-    for i in range(early, nz):
+    second(last)
+    for i in range(early, nz - 1):
         arrive(ret_recv.at[i], (ret_ss, ret_rs), (i,))
     back = ret_recv[early:].reshape(per * block, quarter)
     for tt in range(nt):
@@ -625,7 +655,7 @@
         vmem((nt, nz, chunk, width), BF16),
         vmem((width, 2 * units), BF16),
         vmem((nt, units, quarter), BF16),
-        vmem((nt, nz // 2, nt * 2 * chunk, units), BF16),
+        vmem((nt, nz, nt * chunk, units), BF16),
         vmem((nz, nt * chunk, quarter), BF16),
         vmem((nz, nt * chunk, quarter), BF16),
         vmem((nt * nrow, quarter), F32),
@@ -649,7 +679,8 @@
         (nz,),
         (nz, nt),
         (nz, 2),
-        (nz // 2, nt),
+        (nz, nt),
+        (nz // 2, 2),
         (nz,),
         (nx,),
         (nt,),

time: 141 us -> 134 us (0.950)
  Pallas kernels: 139 us -> 133 us
    pallas_call x1, Pallas kernels: 139 us -> 133 us  [on_device(): pl.pallas_call(functools.partial(kernel, (nx, nz, nc, nt)), out_shape=jax...]
where the time goes in v3:
time: 134 us
  Pallas kernels  133 us (99%)
  local copies, waits for them, and re-layouts  1.47 us (1%)
    pallas_call x1, Pallas kernels, on_device(): pl.pallas_call(functools.partial(kernel, (nx, nz, nc, nt)), out_shape=jax...  133 us

profile of v3, /device:TPU:1, one launch (start us, length us, event | category | flops | bytes accessed | tf_op | source)
XLA Modules:
  0.0 134.1 jit_solution(13762645342939503945)
XLA Ops:
  0.0 132.6 %layer.1 = bf16[8,4096]{1,0:T(8,128)(2,1)} custom-call(s32[32]{0:T(128)} %lengths_ref.1, bf16[32,128]{1,0:T(8,128)(2,1)} %bitcast.21, bf16[32,128]{1,0:T(8,128)(2,1)} %bitcast.22, bf16[32,128]{1,0:T(8,128)(2,1)} %bitcast.23, s32[8,8]{1,0:T(8,128)} %bitcast.24, f32[8,8]{1,0:T(8,128)} %bitcast.25, bf16[32,16,128]{2,1,0:T(8,128)(2,1)} %q_hbm.1, ...), custom_call_target="tpu_custom_call" | custom-call | tf_op jit(solution)/shard_map/layer/pallas_call | solution.py:691
  132.6 1.5 %copy.16 = bf16[1,8,4096]{2,1,0:T(8,128)(2,1)} copy(bf16[1,8,4096]{2,1,0:T(8,128)(2,1)} %bitcast.18) | data formatting | bytes 131072

commit v4 on v3

--- a/solution.py
+++ b/solution.py
@@ -191,7 +191,7 @@
 
     barrier = pltpu.get_barrier_semaphore()
     partners = (
-        [z_peer(d) for d in range(1, nz)]
+        [z_peer(d) for d in (1, -1)]
         + [x_peer(d) for d in range(1, nx)]
         + [sibling]
         + [t_peer(d) for d in range(1, nt)]

time: 134 us -> 135 us (level)
  no operation moved by 1% of the time
where the time goes in v4:
time: 135 us
  Pallas kernels  133 us (99%)
  local copies, waits for them, and re-layouts  1.47 us (1%)
    pallas_call x1, Pallas kernels, on_device(): pl.pallas_call(functools.partial(kernel, (nx, nz, nc, nt)), out_shape=jax...  133 us

profile of v4, /device:TPU:1, one launch (start us, length us, event | category | flops | bytes accessed | tf_op | source)
XLA Modules:
  0.0 135.0 jit_solution(258069028225874590)
XLA Ops:
  0.0 133.5 %layer.1 = bf16[8,4096]{1,0:T(8,128)(2,1)} custom-call(s32[32]{0:T(128)} %lengths_ref.1, bf16[32,128]{1,0:T(8,128)(2,1)} %bitcast.21, bf16[32,128]{1,0:T(8,128)(2,1)} %bitcast.22, bf16[32,128]{1,0:T(8,128)(2,1)} %bitcast.23, s32[8,8]{1,0:T(8,128)} %bitcast.24, f32[8,8]{1,0:T(8,128)} %bitcast.25, bf16[32,16,128]{2,1,0:T(8,128)(2,1)} %q_hbm.1, ...), custom_call_target="tpu_custom_call" | custom-call | tf_op jit(solution)/shard_map/layer/pallas_call | solution.py:691
  133.5 1.5 %copy.16 = bf16[1,8,4096]{2,1,0:T(8,128)(2,1)} copy(bf16[1,8,4096]{2,1,0:T(8,128)(2,1)} %bitcast.18) | data formatting | bytes 131072

commit v5 on v3

--- a/solution.py
+++ b/solution.py
@@ -577,7 +577,7 @@
                 fin_send[cc, xx, tt * rows : (tt + 1) * rows, :] = part[xx, cc]
     send(fin_send.at[1 - c], fin_pair, (fin_ss, fin_rs), (0,), sibling)
     arrive(fin_pair, (fin_ss, fin_rs), (0,))
-    for d in range(1, nx):
+    for d in sorted(range(1, nx), key=lambda d: -min(d, nx - d)):
         p = x_index(d)
         fin_sum[p] = (fin_send[c, p].astype(F32) + fin_pair[p].astype(F32)).astype(BF16)
         send(fin_sum.at[p], fin_recv.at[x], (fin_ss, fin_rs), (d,), x_peer(d))
@@ -588,7 +588,7 @@
         total = total + fin_recv[p].astype(F32)
     for tt in range(nt):
         fy_send[tt] = total[tt * rows : (tt + 1) * rows]
-    for d in range(1, nt):
+    for d in sorted(range(1, nt), key=lambda d: -min(d, nt - d)):
         send(fy_send.at[t_index(d)], fy_recv.at[t], (fy_ss, fy_rs), (d,), t_peer(d))
     fy_recv[t] = fy_send[t]
     for d in range(1, nt):

time: 134 us -> 133 us (level)
  Pallas kernels: 133 us -> 131 us
where the time goes in v5:
time: 133 us
  Pallas kernels  131 us (98%)
  local copies, waits for them, and re-layouts  1.47 us (1%)
    pallas_call x1, Pallas kernels, on_device(): pl.pallas_call(functools.partial(kernel, (nx, nz, nc, nt)), out_shape=jax...  131 us

profile of v5, /device:TPU:1, one launch (start us, length us, event | category | flops | bytes accessed | tf_op | source)
XLA Modules:
  0.0 132.9 jit_solution(11901913286282046377)
XLA Ops:
  0.0 131.4 %layer.1 = bf16[8,4096]{1,0:T(8,128)(2,1)} custom-call(s32[32]{0:T(128)} %lengths_ref.1, bf16[32,128]{1,0:T(8,128)(2,1)} %bitcast.21, bf16[32,128]{1,0:T(8,128)(2,1)} %bitcast.22, bf16[32,128]{1,0:T(8,128)(2,1)} %bitcast.23, s32[8,8]{1,0:T(8,128)} %bitcast.24, f32[8,8]{1,0:T(8,128)} %bitcast.25, bf16[32,16,128]{2,1,0:T(8,128)(2,1)} %q_hbm.1, ...), custom_call_target="tpu_custom_call" | custom-call | tf_op jit(solution)/shard_map/layer/pallas_call | solution.py:691
  131.4 1.5 %copy.16 = bf16[1,8,4096]{2,1,0:T(8,128)(2,1)} copy(bf16[1,8,4096]{2,1,0:T(8,128)(2,1)} %bitcast.18) | data formatting | bytes 131072
